TPU v7x, 512 devices: a whole 4x8x8 slice. The times are simulated.
512 devices in a mesh: blk: 16 (over z, y_hi), pair: 32 (over y_lo, x, core).
Axes of the slice: x: 4, y: 8 (y_hi: 2, y_lo: 4; y = y_hi * 4 + y_lo), z: 8, core: 2. Of those that a mesh axis runs over, the one named last changes fastest.
Arguments:
- integrals: float32 [16, 32, 25, 25600], P('blk', 'pair'), may hold values from -0.0390625 to 0.0390625
- amplitudes: float32 [25600, 256], P('blk'), may hold values from -6 to 6
- block_map: int32 [16, 32, 2], P('blk', 'pair'), may hold values from 0 to 31, as said below
- eps_vir: float32 [160], replicated, may hold values from 0.2 to 2
- eps_occ: float32 [16], replicated, may hold values from -1.5 to -0.1
Outputs:
- update: float32 [16, 32, 25, 256], P('blk', 'pair')
Inputs may be any that keep to these rules, and one draw needn't show every extreme that they name: `block_map`: each device's two blocks differ; the device whose pair index differs by 32/2 (same blk index) holds the same two blocks in swapped order; no two devices hold the same ordered pair of blocks. `eps_vir`: the virtual energies are positive and the occupied ones negative, so every denominator is 0.6 or more.
All inputs are finite; a program needn't handle non-finite values.
Results may differ from a plain program's by a relative error of at most 0.00011.
Values sent between devices are 32-bit elements; how exact they have to be, the bound alone decides.
A program may use at most 128 MiB of HBM per device.

v0:
```python
import jax
import jax.numpy as jnp
from jax import lax
from jax.sharding import PartitionSpec as P

OCCUPIED = 16
BLOCK_SIDE = 5


def swapped(block, axis, bit):
    count = lax.axis_size(axis)
    route = []
    for low in range(count):
        high = low | 1 << bit
        if high != low and high < count:
            route += [(low, high), (high, low)]
    return lax.ppermute(block, axis, route)


def lookup(table, index):
    positions = jnp.arange(table.shape[0], dtype=jnp.int32)
    return jnp.sum(jnp.where(index[:, None] == positions[None, :], table[None, :], 0.0), axis=1)


def body(integrals, amplitudes, block_map, eps_vir, eps_occ):
    rows = integrals.shape[2]
    width = integrals.shape[3]
    occ_cols = amplitudes.shape[1]
    local = integrals.reshape(rows, width)
    groups = lax.axis_size("blk")
    block_cols = width // groups
    spread = local.reshape(rows, groups, block_cols)
    arrived = lax.all_to_all(spread, "blk", split_axis=1, concat_axis=1, tiled=True)
    terms = jnp.einsum(
        "rkc,cj->krj",
        arrived,
        amplitudes,
        precision=lax.Precision.HIGHEST,
        preferred_element_type=jnp.float32,
    )
    ladder = lax.psum_scatter(
        terms.reshape(lax.axis_size("blk") * rows, occ_cols), "blk", scatter_dimension=0, tiled=True
    )
    top_bit = lax.axis_size("pair").bit_length() - 2
    partner = swapped(ladder, "pair", top_bit)
    mirrored = (
        partner.reshape(BLOCK_SIDE, BLOCK_SIDE, OCCUPIED, OCCUPIED)
        .transpose(1, 0, 3, 2)
        .reshape(rows, occ_cols)
    )
    blocks = block_map.reshape(2)
    offsets = jnp.arange(BLOCK_SIDE, dtype=jnp.int32)
    energy_a = lookup(eps_vir, blocks[0] * BLOCK_SIDE + offsets)
    energy_b = lookup(eps_vir, blocks[1] * BLOCK_SIDE + offsets)
    denominator = (
        energy_a[:, None, None, None] + energy_b[None, :, None, None] - eps_occ[:, None] - eps_occ
    )
    update = (ladder + mirrored) / denominator.reshape(rows, occ_cols)
    return update.reshape(1, 1, rows, occ_cols)


def solution(mesh):
    in_specs = (P("blk", "pair", None, None), P("blk", None), P("blk", "pair", None), P(), P())
    out_specs = P("blk", "pair", None, None)
    return jax.shard_map(body, mesh=mesh, in_specs=in_specs, out_specs=out_specs, check_vma=False)
```

profile of v0, /device:TPU:22, one launch (start us, length us, event | category | flops | bytes accessed | tf_op | source)
XLA Modules:
  0.0 266.0 jit_solution(13700093351278667481)
XLA Ops:
  0.0 0.0 copy-start
  0.0 9.6 %reduce = f32[25,25600]{1,0:T(8,128)} reduce(f32[1,1,25,25600]{3,1,2,0:T(1,128)} %param.5, f32[]{:T(128)} %constant.12), dimensions={0,1}, to_apply=%param.5.reduce_sub_computation | reduce | bytes 5120004 | tf_op args[0]
  9.6 3.6 %reshape_reshape.3 = f32[25,16,1600]{2,1,0:T(8,128)} reshape(f32[25,25600]{1,0:T(8,128)} %reduce) | data formatting | bytes 5120000 | tf_op jit(solution)/shard_map/reshape;reshape | solution.py:32
  13.2 4.4 %copy.13 = f32[25,16,1600]{2,0,1:T(8,128)} copy(f32[25,16,1600]{2,1,0:T(8,128)} %reshape_reshape.3) | data formatting | bytes 5120000 | tf_op jit(solution)/shard_map/reshape;reshape | solution.py:32
  17.6 0.0 copy-start.2
  17.6 0.0 copy-start.3
  17.6 14.1 %all-to-all-start = ((f32[25,16,1600]{2,0,1:T(8,128)}), f32[25,16,1600]{2,0,1:T(8,128)}, u32[]{:S(2)}, u32[]{:S(2)}) async-start(f32[25,16,1600]{2,0,1:T(8,128)} %copy.13), calls=%async_computation | async-start | bytes 6815744 | tf_op jit(solution)/shard_map/all_to_all | solution.py:33
  31.7 0.0 copy-done.2
  31.7 0.6 fusion.6
  33.6 0.0 copy-done.3
  33.6 0.2 select_reduce_fusion.1
  33.8 0.0 copy-start.1
  33.8 121.4 %all-to-all-done = f32[25,16,1600]{2,0,1:T(8,128)} async-done(((f32[25,16,1600]{2,0,1:T(8,128)}), f32[25,16,1600]{2,0,1:T(8,128)}, u32[]{:S(2)}, u32[]{:S(2)}) %all-to-all-start) | async-done | bytes 2560032 | tf_op jit(solution)/shard_map/all_to_all | solution.py:33
  155.2 0.0 copy-done
  155.2 5.0 %fusion.3 = f32[16,25,256]{2,1,0:T(8,128)S(1)} fusion(f32[25,16,1600]{2,0,1:T(8,128)} %all-to-all-done, f32[1600,256]{1,0:T(8,128)S(1)} %copy-done), kind=kOutput, calls=%fused_computation.2 | convolution fusion | flops 1966080000 | bytes 4608000 | tf_op jit(solution)/shard_map/rkc,cj->krj/dot_general | solution.py:34
  160.2 0.1 reshape.73
  160.3 75.2 %fusion = f32[32,256]{1,0:T(8,128)S(1)} fusion(f32[400,256]{1,0:T(8,128)S(1)} %reshape.73), kind=kCustom, calls=%all-reduce-scatter | all-reduce-scatter fusion | flops 131073 | bytes 444416
  235.5 1.9 collective-permute-start.1
  237.4 4.3 %collective-permute-start.2 = (f32[32,256]{1,0:T(8,128)S(1)}, f32[32,256]{1,0:T(8,128)S(1)}, u32[]{:S(2)}, u32[]{:S(2)}) collective-permute-start(f32[32,256]{1,0:T(8,128)S(1)} %fusion), channel_id=1, source_target_pairs={{0,64},{32,96},{64,128},{96,160},{128,192},{160,224},{192,256},{22... | collective-permute-start | bytes 98312
  241.7 9.2 %collective-permute-start.3 = (f32[32,256]{1,0:T(8,128)S(1)}, f32[32,256]{1,0:T(8,128)S(1)}, u32[]{:S(2)}, u32[]{:S(2)}) collective-permute-start(f32[32,256]{1,0:T(8,128)S(1)} %fusion), channel_id=1, source_target_pairs={{0,96},{32,128},{64,160},{96,192},{128,224},{160,256},{192,288},{2... | collective-permute-start | bytes 98312
  250.9 4.7 %collective-permute-start.4 = (f32[9,256]{1,0:T(8,128)S(1)}, f32[9,256]{1,0:T(8,128)S(1)}, u32[]{:S(2)}, u32[]{:S(2)}) collective-permute-start(f32[9,256]{1,0:T(8,128)S(1)} %slice.10), channel_id=1, source_target_pairs={{0,128},{32,160},{64,192},{96,224},{128,256},{160,288},{192,320},{... | collective-permute-start | bytes 27656
  255.7 0.1 broadcast_add_fusion
  255.7 1.3 dynamic-slice.4
  257.6 0.0 collective-permute-done.4
  257.7 0.0 collective-permute-done.1
  257.7 0.0 collective-permute-done.2
  257.7 0.0 collective-permute-done.3
  257.7 0.6 concatenate
  258.3 1.9 collective-permute-start
  260.2 0.0 copy-done.1
  260.2 0.1 broadcast_subtract_fusion
  260.3 0.1 sub.41
  260.4 0.1 sub.42
  260.6 0.1 sub.44
  260.6 4.3 %collective-permute-done = f32[25,256]{1,0:T(8,128)S(1)} collective-permute-done((f32[25,256]{1,0:T(8,128)S(1)}, f32[25,256]{1,0:T(8,128)S(1)}, u32[]{:S(2)}, u32[]{:S(2)}) %collective-permute-start) | collective-permute-done | bytes 25632 | tf_op jit(solution)/shard_map/ppermute | solution.py:17
  265.0 0.1 reshape.74
  265.1 0.1 copy.14
  265.2 0.1 reshape.75
  265.4 0.6 copy.15
  (5 shorter events, 0.0 us)
Async XLA Ops:
  0.0 155.2 %copy-start = (f32[1600,256]{1,0:T(8,128)S(1)}, f32[1600,256]{1,0:T(8,128)}, u32[]{:S(2)}) copy-start(f32[1600,256]{1,0:T(8,128)} %param.6) | copy-start | bytes 4915204
  17.6 14.1 %copy-start.2 = (s32[1,1,2]{2,1,0:T(1,128)S(1)}, s32[1,1,2]{2,1,0:T(1,128)}, u32[]{:S(2)}) copy-start(s32[1,1,2]{2,1,0:T(1,128)} %param.7) | copy-start | bytes 28
  17.6 16.0 %copy-start.3 = (f32[160]{0:T(256)S(1)}, f32[160]{0:T(256)}, u32[]{:S(2)}) copy-start(f32[160]{0:T(256)} %param.8) | copy-start | bytes 1924
  17.6 137.6 %all-to-all-start = ((f32[25,16,1600]{2,0,1:T(8,128)}), f32[25,16,1600]{2,0,1:T(8,128)}, u32[]{:S(2)}, u32[]{:S(2)}) async-start(f32[25,16,1600]{2,0,1:T(8,128)} %copy.13), calls=%async_computation | async-start | bytes 6815744 | tf_op jit(solution)/shard_map/all_to_all | solution.py:33
  33.8 226.4 %copy-start.1 = (f32[16]{0:T(128)S(1)}, f32[16]{0:T(128)}, u32[]{:S(2)}) copy-start(f32[16]{0:T(128)} %param.9) | copy-start | bytes 196
  235.5 22.2 %collective-permute-start.1 = (f32[32,256]{1,0:T(8,128)S(1)}, f32[32,256]{1,0:T(8,128)S(1)}, u32[]{:S(2)}, u32[]{:S(2)}) collective-permute-start(f32[32,256]{1,0:T(8,128)S(1)} %fusion), channel_id=1, source_target_pairs={{0,32},{32,64},{64,96},{96,128},{128,160},{160,192},{192,224},{224... | collective-permute-start | bytes 98312
  237.4 20.3 %collective-permute-start.2 = (f32[32,256]{1,0:T(8,128)S(1)}, f32[32,256]{1,0:T(8,128)S(1)}, u32[]{:S(2)}, u32[]{:S(2)}) collective-permute-start(f32[32,256]{1,0:T(8,128)S(1)} %fusion), channel_id=1, source_target_pairs={{0,64},{32,96},{64,128},{96,160},{128,192},{160,224},{192,256},{22... | collective-permute-start | bytes 98312
  241.7 16.0 %collective-permute-start.3 = (f32[32,256]{1,0:T(8,128)S(1)}, f32[32,256]{1,0:T(8,128)S(1)}, u32[]{:S(2)}, u32[]{:S(2)}) collective-permute-start(f32[32,256]{1,0:T(8,128)S(1)} %fusion), channel_id=1, source_target_pairs={{0,96},{32,128},{64,160},{96,192},{128,224},{160,256},{192,288},{2... | collective-permute-start | bytes 98312
  250.9 6.7 %collective-permute-start.4 = (f32[9,256]{1,0:T(8,128)S(1)}, f32[9,256]{1,0:T(8,128)S(1)}, u32[]{:S(2)}, u32[]{:S(2)}) collective-permute-start(f32[9,256]{1,0:T(8,128)S(1)} %slice.10), channel_id=1, source_target_pairs={{0,128},{32,160},{64,192},{96,224},{128,256},{160,288},{192,320},{... | collective-permute-start | bytes 27656
  258.3 6.7 %collective-permute-start = (f32[25,256]{1,0:T(8,128)S(1)}, f32[25,256]{1,0:T(8,128)S(1)}, u32[]{:S(2)}, u32[]{:S(2)}) collective-permute-start(f32[25,256]{1,0:T(8,128)S(1)} %constant_dynamic-slice_fusion), channel_id=1, source_target_pairs={{0,16},{16,0},{1,17},{17,1},{2,18},{18,2},{3,19},{19,3},{4,20},{20... | collective-permute-start | bytes 76808 | tf_op jit(solution)/shard_map/ppermute | solution.py:17
where the time goes:
time: 267 us; the launch traced here: 266 us
  waiting for transfers between devices  126 us (47%)
  blocking collectives  75.2 us (28%)
  starting transfers between devices  36.1 us (14%)
  local copies, waits for them, and re-layouts  11.8 us (4%)
  other arithmetic  10 us (4%)
  matrix products  5.01 us (2%)
    all_to_all x1, waiting for transfers between devices, body(): lax.all_to_all(spread, 'blk', split_axis=1, concat_axis=1, tiled=True)  121 us
    unnamed x1, blocking collectives  75.2 us
    unnamed x4, starting transfers between devices  20.1 us
    all_to_all x1, starting transfers between devices, body(): lax.all_to_all(spread, 'blk', split_axis=1, concat_axis=1, tiled=True)  14.1 us
    unnamed x1, other arithmetic  9.63 us
    another operation x2, local copies, waits for them, and re-layouts, body(): spread = local.reshape(rows, groups, block_cols)  7.97 us
  transfers between devices with their start and end apart: 6, of which 2 were waited for; matrix products, arithmetic and copies ran while one was open for 1% of the time, Pallas kernels for 0%

commit v1 on v0

v1 whole, which is shorter than its diff:
```python
import functools

import jax
import jax.numpy as jnp
from jax import lax
from jax.experimental import pallas as pl
from jax.experimental.pallas import tpu as pltpu
from jax.sharding import PartitionSpec as P

MESH = pl.DeviceIdType.MESH

OCCUPIED = 16
SIDE = 5
ROWS = 25
FULL = 24
SLOT = 32
COLS = 256
WINDOW = 3200
MAIN = 192
EXTRA = 8
HALF = 96
FIRST = EXTRA + HALF
PIECE = FIRST + HALF
X, Y, Z = 4, 8, 8
SENDS = ((2, 1, 0), (6, -1, 0), (3, 0, 1), (5, 0, -1), (1, -1, 1), (7, 1, -1), (4, 2, 0))
CHUNKS = ((0, FIRST), (FIRST, HALF))


def device(z, y, x, core):
    return (z * 2 + y // 4, (y % 4) * 8 + x * 2 + core)


def kernel(
    v_ref, t_ref, map_ref, vir_ref, occ_ref, out_ref,
    vbuf, last, packed, vlast, tbuf, acc, give, parts, mine, other, den, turn,
    tin_send, tin_recv, ring_send, ring_recv, core_send, core_recv,
    v_send, v_recv, v_own, last_send, last_recv, last_own, part_send, part_recv, mir_send, mir_recv,
):
    blk, pair = lax.axis_index("blk"), lax.axis_index("pair")
    z, y_hi = blk // 2, blk % 2
    y_lo, x, core = pair // 8, (pair // 2) % 4, pair % 2
    y = y_hi * 4 + y_lo
    colour = (3 * z + 2 * x + 1) % 8

    def at(dx=0, dy=0, dz=0):
        return device((z + dz + Z) % Z, (y + dy + Y) % Y, (x + dx + X) % X, core)

    sibling = device(z, y, x, 1 - core)
    up, down = at(dy=1), at(dy=-1)
    twin = device(z, y_hi * 4 + (y_lo + 2) % 4, x, core)
    source = device(colour, y, x, core)
    target = device((3 * (z - 2 * x - 1) + 72) % 8, y, x, core)

    last_row = pltpu.make_async_copy(v_ref.at[0, 0, pl.ds(FULL, 1), :], last, last_own.at[0])
    last_row.start()

    barrier = pltpu.get_barrier_semaphore()
    greet = [sibling, up, down, twin, source] + [at(dx=-dx, dz=-dz) for _, dx, dz in SENDS]
    for peer in greet:
        pl.semaphore_signal(barrier, inc=1, device_id=peer, device_id_type=MESH)
    pl.semaphore_wait(barrier, len(greet))

    def remote(src, dst, send, recv, peer):
        return pltpu.make_async_remote_copy(
            src_ref=src, dst_ref=dst, send_sem=send, recv_sem=recv, device_id=peer, device_id_type=MESH
        )

    main_at = pl.multiple_of(y_hi * 64 + y_lo * 384 + core * MAIN, 8)
    extra_at = pl.multiple_of((1 - y_hi) * 1536 + 8 * (2 * y_lo + core), 8)
    home = tbuf.at[y, core]
    tin = [
        remote(t_ref.at[pl.ds(extra_at, EXTRA)], home.at[pl.ds(0, EXTRA)], tin_send.at[0], tin_recv.at[0], target),
        remote(t_ref.at[pl.ds(main_at, HALF)], home.at[pl.ds(EXTRA, HALF)], tin_send.at[1], tin_recv.at[1], target),
        remote(
            t_ref.at[pl.ds(pl.multiple_of(main_at + HALF, 8), HALF)], home.at[pl.ds(FIRST, HALF)],
            tin_send.at[2], tin_recv.at[2], target,
        ),
    ]
    for copy in tin:
        copy.start()

    def columns(step):
        return pl.ds(pl.multiple_of(((colour + step) % 8) * WINDOW, 128), WINDOW)

    vout = []
    for i, (step, dx, dz) in enumerate(SENDS):
        vout.append(
            remote(
                v_ref.at[0, 0, pl.ds(0, FULL), columns(step)], vbuf.at[i + 1],
                v_send.at[i], v_recv.at[i], at(dx=dx, dz=dz),
            )
        )
    for copy in vout:
        copy.start()
    own = pltpu.make_async_copy(v_ref.at[0, 0, pl.ds(0, FULL), columns(0)], vbuf.at[0], v_own.at[0])
    own.start()

    last_row.wait()
    for k in range(8):
        for j in range(25):
            packed[k, j : j + 1, :] = last[0:1, (25 * k + j) * 128 : (25 * k + j + 1) * 128]
    for i, (step, dx, dz) in enumerate(SENDS):
        copy = remote(
            packed.at[(colour + step) % 8], vlast.at[i + 1], last_send.at[i], last_recv.at[i], at(dx=dx, dz=dz)
        )
        copy.start()
        vout.append(copy)
    vlast[0] = packed[colour]

    lane = lax.broadcasted_iota(jnp.int32, (1, COLS), 1)
    occ_i = jnp.zeros((1, COLS), jnp.float32)
    occ_j = jnp.zeros((1, COLS), jnp.float32)
    for i in range(OCCUPIED):
        occ_i = jnp.where(lane // OCCUPIED == i, occ_ref[i], occ_i)
        occ_j = jnp.where(lane % OCCUPIED == i, occ_ref[i], occ_j)
    for s in range(SIDE):
        for t in range(SIDE):
            both = vir_ref[map_ref[0, 0, 0] * SIDE + s] + vir_ref[map_ref[0, 0, 1] * SIDE + t]
            r = s * SIDE + t
            den[r : r + 1, :] = (both - occ_i) - occ_j
    row = lax.broadcasted_iota(jnp.int32, (COLS, COLS), 0)
    col = lax.broadcasted_iota(jnp.int32, (COLS, COLS), 1)
    turn[...] = ((row // OCCUPIED == col % OCCUPIED) & (row % OCCUPIED == col // OCCUPIED)).astype(jnp.bfloat16)

    started = []

    def ring(way, hop, chunk):
        at_y = (y - hop + Y) % Y if way == 0 else (y + hop) % Y
        start, size = CHUNKS[chunk]
        ref = tbuf.at[at_y, core, pl.ds(start, size)]
        return remote(ref, ref, ring_send.at[way, hop, chunk], ring_recv.at[way, hop, chunk], up if way == 0 else down)

    def arrived(way, hop, chunk):
        at_y = (y - hop - 1 + Y) % Y if way == 0 else (y + hop + 1) % Y
        start, size = CHUNKS[chunk]
        ref = tbuf.at[at_y, core, pl.ds(start, size)]
        return remote(ref, ref, ring_send.at[way, hop, chunk], ring_recv.at[way, hop, chunk], up if way == 0 else down)

    def place_y(place):
        step = (0, -1, -2, -3, 1, 2, 3, 4)[place]
        return (y + step + Y) % Y

    def across(place, chunk):
        start, size = CHUNKS[chunk]
        ref = tbuf.at[place_y(place), core, pl.ds(start, size)]
        return remote(ref, ref, core_send.at[place, chunk], core_recv.at[place, chunk], sibling)

    def across_in(place, chunk):
        start, size = CHUNKS[chunk]
        ref = tbuf.at[place_y(place), 1 - core, pl.ds(start, size)]
        return remote(ref, ref, core_send.at[place, chunk], core_recv.at[place, chunk], sibling)

    def go(copy):
        copy.start()
        started.append(copy)

    for chunk in range(2):
        for copy in (tin[:2], tin[2:])[chunk]:
            copy.wait_recv()
        go(ring(0, 0, chunk))
        go(ring(1, 0, chunk))
        go(across(0, chunk))
    for hop in range(1, 4):
        for chunk in range(2):
            for way in range(2):
                arrived(way, hop - 1, chunk).wait_recv()
                if hop < 3 or way == chunk:
                    go(ring(way, hop, chunk))
                go(across(hop + 3 * way, chunk))
    for way in range(2):
        arrived(way, 3, way).wait_recv()
        go(across(7, way))

    own.wait()
    for copy in vout:
        copy.wait_recv()

    def split(value):
        high = value.astype(jnp.bfloat16)
        return high, (value - high.astype(jnp.float32)).astype(jnp.bfloat16)

    def product(v, t):
        v_high, v_low = split(v)
        t_high, t_low = split(t)
        dot = functools.partial(jnp.dot, preferred_element_type=jnp.float32)
        return dot(v_high, t_high) + (dot(v_low, t_high) + dot(v_high, t_low))

    def gathered(tile, tiles):
        first = pl.multiple_of(128 * tile, 128)
        v = vbuf[:, :, pl.ds(first, 128 * tiles)].reshape(8 * FULL, 128 * tiles)
        ends = [vlast[:, pl.ds(tile + k, 1), :].reshape(8, 128) for k in range(tiles)]
        return jnp.concatenate([v, jnp.concatenate(ends, axis=1)], axis=0)

    for place in (0, 1, 4, 2, 5, 3, 6, 7):
        for chunk in range(2):
            across_in(place, chunk).wait_recv()
        at_y = place_y(place)
        first = pl.multiple_of(384 * at_y + 128 * (at_y // 4), 128)
        t = tbuf[at_y, :, EXTRA:PIECE, :].reshape(2 * MAIN, COLS)
        tile = 3 * at_y + at_y // 4
        v = gathered(tile, 3)
        if place == 0:
            acc[...] = product(v, t)
        else:
            acc[...] += product(v, t)
    t = tbuf[:, :, 0:EXTRA, :].reshape(128, COLS)
    acc[...] += product(gathered(12, 1), t)

    back = []
    for i, (_, dx, dz) in enumerate(SENDS):
        give[i, 0:FULL, :] = acc[FULL * (i + 1) : FULL * (i + 2), :]
        give[i, FULL:ROWS, :] = acc[8 * FULL + i + 1 : 8 * FULL + i + 2, :]
        copy = remote(give.at[i], parts.at[i], part_send.at[i], part_recv.at[i], at(dx=-dx, dz=-dz))
        copy.start()
        back.append(copy)
    total = jnp.concatenate([acc[0:FULL, :], acc[8 * FULL : 8 * FULL + 8, :]], axis=0)
    for i in range(7):
        back[i].wait_recv()
        total = total + parts[i]
    mine[...] = total
    swap = remote(mine, other, mir_send.at[0], mir_recv.at[0], twin)
    swap.start()
    swap.wait_recv()
    dot = functools.partial(jnp.dot, preferred_element_type=jnp.float32)
    high, rest = split(other[...])
    mid = (other[...] - high.astype(jnp.float32)) - rest.astype(jnp.float32)
    turned = (dot(high, turn[...]) + dot(rest, turn[...])) + dot(mid.astype(jnp.bfloat16), turn[...])
    for s in range(SIDE):
        for t in range(SIDE):
            r, q = s * SIDE + t, t * SIDE + s
            out_ref[0, 0, r : r + 1, :] = (total[r : r + 1] + turned[q : q + 1]) / den[r : r + 1, :]

    for copy in tin + vout + started + back + [swap]:
        copy.wait_send()


def body(integrals, amplitudes, block_map, eps_vir, eps_occ):
    smem = pl.BlockSpec(memory_space=pltpu.SMEM)
    hbm = pl.BlockSpec(memory_space=pl.ANY)
    dma = pltpu.SemaphoreType.DMA
    f32 = jnp.float32
    return pl.pallas_call(
        kernel,
        out_shape=jax.ShapeDtypeStruct((1, 1, ROWS, COLS), f32),
        in_specs=[hbm, hbm, smem, smem, smem],
        out_specs=pl.BlockSpec(memory_space=pltpu.VMEM),
        scratch_shapes=[
            pltpu.VMEM((8, FULL, WINDOW), f32),
            pltpu.VMEM((1, 8 * WINDOW), f32),
            pltpu.VMEM((8, SLOT, 128), f32),
            pltpu.VMEM((8, SLOT, 128), f32),
            pltpu.VMEM((8, 2, PIECE, COLS), f32),
            pltpu.VMEM((8 * ROWS, COLS), f32),
            pltpu.VMEM((7, SLOT, COLS), f32),
            pltpu.VMEM((7, SLOT, COLS), f32),
            pltpu.VMEM((SLOT, COLS), f32),
            pltpu.VMEM((SLOT, COLS), f32),
            pltpu.VMEM((SLOT, COLS), f32),
            pltpu.VMEM((COLS, COLS), jnp.bfloat16),
            dma((3,)), dma((3,)),
            dma((2, 4, 2)), dma((2, 4, 2)),
            dma((8, 2)), dma((8, 2)),
            dma((7,)), dma((7,)), dma((1,)),
            dma((7,)), dma((7,)), dma((1,)),
            dma((7,)), dma((7,)),
            dma((1,)), dma((1,)),
        ],
        compiler_params=pltpu.CompilerParams(
            collective_id=0, has_side_effects=True, vmem_limit_bytes=40 * 2**20
        ),
        name="ladder",
    )(integrals, amplitudes, block_map, eps_vir, eps_occ)


def solution(mesh):
    in_specs = (P("blk", "pair", None, None), P("blk", None), P("blk", "pair", None), P(), P())
    out_specs = P("blk", "pair", None, None)
    return jax.shard_map(body, mesh=mesh, in_specs=in_specs, out_specs=out_specs, check_vma=False)
```

time: 267 us -> 56.6 us (0.21)
  the two profiles are of different devices: /device:TPU:22 before, /device:TPU:2 now
where the time goes in v1:
time: 56.6 us; the launch traced here: 56.5 us
  Pallas kernels  53.4 us (94%)
  local copies, waits for them, and re-layouts  3.03 us (5%)
    pallas_call x1, Pallas kernels, body(): pl.pallas_call(kernel, out_shape=jax.ShapeDtypeStruct((1, 1, ROWS, COLS),...  53.4 us
    unnamed x9, local copies, waits for them, and re-layouts  2.39 us

profile of v1, /device:TPU:2, one launch (start us, length us, event | category | flops | bytes accessed | tf_op | source)
XLA Modules:
  0.0 56.5 jit_solution(15832117031919013570)
XLA Ops:
  0.0 0.0 copy-start.3
  0.0 0.0 copy-start.1
  0.0 0.0 copy-start.2
  0.0 0.0 copy-start
  0.0 2.4 %copy.6.v_ref = f32[1,1,25,25600]{3,2,1,0:T(8,128)S(1)} copy(f32[1,1,25,25600]{3,1,2,0:T(1,128)} %param.5) | data formatting | bytes 5120000 | tf_op args[0]
  2.4 0.0 copy-done.3
  2.4 0.0 copy-done.1
  2.4 0.0 copy-done.2
  2.4 0.0 copy-done
  2.4 53.4 %ladder.1 = f32[1,1,25,256]{3,2,1,0:T(8,128)S(1)} custom-call(f32[1,1,25,25600]{3,2,1,0:T(8,128)S(1)} %copy.6.v_ref, f32[1600,256]{1,0:T(8,128)S(1)} %copy-done, s32[1,1,2]{2,1,0:T(1,128)S(1)} %copy-done.2, f32[160]{0:T(256)S(1)} %copy-done.1, f32[16]{0:T(128)S(1)} %copy-done.3), custom_call_target="tpu_custom_call" | custom-call | tf_op jit(solution)/shard_map/ladder/pallas_call | solution.py:242
  55.8 0.6 %copy.7 = f32[1,1,25,256]{3,1,2,0:T(1,128)} copy(f32[1,1,25,256]{3,2,1,0:T(8,128)S(1)} %ladder.1) | data formatting | bytes 51200 | tf_op jit(solution)/shard_map/ladder/pallas_call | solution.py:242
Async XLA Ops:
  0.0 2.4 %copy-start.3 = (f32[16]{0:T(128)S(1)}, f32[16]{0:T(128)}, u32[]{:S(2)}) copy-start(f32[16]{0:T(128)} %occ_ref.1) | copy-start | bytes 196
  0.0 2.4 %copy-start.1 = (f32[160]{0:T(256)S(1)}, f32[160]{0:T(256)}, u32[]{:S(2)}) copy-start(f32[160]{0:T(256)} %vir_ref.1) | copy-start | bytes 1924
  0.0 2.4 %copy-start.2 = (s32[1,1,2]{2,1,0:T(1,128)S(1)}, s32[1,1,2]{2,1,0:T(1,128)}, u32[]{:S(2)}) copy-start(s32[1,1,2]{2,1,0:T(1,128)} %map_ref.1) | copy-start | bytes 28
  0.0 2.4 %copy-start = (f32[1600,256]{1,0:T(8,128)S(1)}, f32[1600,256]{1,0:T(8,128)}, u32[]{:S(2)}) copy-start(f32[1600,256]{1,0:T(8,128)} %t_ref.1) | copy-start | bytes 4915204

commit v2 on v1

v2 whole, which is shorter than its diff:
```python
import functools

import jax
import jax.numpy as jnp
from jax import lax
from jax.experimental import pallas as pl
from jax.experimental.pallas import tpu as pltpu
from jax.sharding import PartitionSpec as P

MESH = pl.DeviceIdType.MESH

OCCUPIED = 16
SIDE = 5
ROWS = 25
SLOT = 32
LANES = 128
TILES = 25
COLS = 256
MAIN = 192
EXTRA = 8
PIECE = EXTRA + MAIN
X, Y, Z = 4, 8, 8
SENDS = ((2, 1, 0), (6, -1, 0), (3, 0, 1), (5, 0, -1), (1, -1, 1), (7, 1, -1), (4, 2, 0))
CHUNKS = ((0, 56), (56, 48), (104, 48), (152, 48))
LAST_WAY = (0, 0, 1, 1)


def device(z, y, x, core):
    return (z * 2 + y // 4, (y % 4) * 8 + x * 2 + core)


def kernel(
    v_ref, t_ref, map_ref, vir_ref, occ_ref, out_ref,
    vbuf, tbuf, acc, give, parts, mine, other, den, turn,
    tin_send, tin_recv, ring_send, ring_recv, core_send, core_recv,
    v_send, v_recv, v_own, part_send, part_recv, mir_send, mir_recv,
):
    blk, pair = lax.axis_index("blk"), lax.axis_index("pair")
    z, y_hi = blk // 2, blk % 2
    y_lo, x, core = pair // 8, (pair // 2) % 4, pair % 2
    y = y_hi * 4 + y_lo
    colour = (3 * z + 2 * x + 1) % 8

    def at(dx=0, dy=0, dz=0):
        return device((z + dz + Z) % Z, (y + dy + Y) % Y, (x + dx + X) % X, core)

    sibling = device(z, y, x, 1 - core)
    up, down = at(dy=1), at(dy=-1)
    mirror = 2 - 4 * (y_lo // 2)
    twin = at(dy=mirror)
    source = device(colour, y, x, core)
    target = device((3 * (z - 2 * x - 1) + 72) % 8, y, x, core)

    barrier = pltpu.get_barrier_semaphore()
    greet = [sibling, up, down, twin, source] + [at(dx=-dx, dz=-dz) for _, dx, dz in SENDS]
    for peer in greet:
        pl.semaphore_signal(barrier, inc=1, device_id=peer, device_id_type=MESH)
    pl.semaphore_wait(barrier, len(greet))

    def remote(src, dst, send, recv, peer):
        return pltpu.make_async_remote_copy(
            src_ref=src, dst_ref=dst, send_sem=send, recv_sem=recv, device_id=peer, device_id_type=MESH
        )

    main_at = pl.multiple_of(y_hi * 64 + y_lo * 384 + core * MAIN, 8)
    extra_at = pl.multiple_of((1 - y_hi) * 1536 + 8 * (2 * y_lo + core), 8)
    home = tbuf.at[y, core]
    tin = [
        remote(t_ref.at[pl.ds(extra_at, EXTRA)], home.at[pl.ds(0, EXTRA)], tin_send.at[4], tin_recv.at[4], target)
    ]
    for chunk, (start, size) in enumerate(CHUNKS):
        skip = EXTRA if chunk == 0 else 0
        rows = pl.ds(pl.multiple_of(main_at + (start + skip - EXTRA), 8), size - skip)
        tin.append(
            remote(t_ref.at[rows], home.at[pl.ds(start + skip, size - skip)], tin_send.at[chunk], tin_recv.at[chunk], target)
        )
    for n, copy in enumerate(tin):
        copy.start()
    slots = vbuf.reshape(8, ROWS, TILES, 1, LANES)

    def columns(step):
        return v_ref.at[:, pl.ds(((colour + step) % 8) * TILES, TILES)]

    vout = []
    for i, (step, dx, dz) in enumerate(SENDS):
        vout.append(remote(columns(step), slots.at[i + 1], v_send.at[i], v_recv.at[i], at(dx=dx, dz=dz)))
    for copy in vout:
        copy.start()
    own = pltpu.make_async_copy(columns(0), slots.at[0], v_own.at[0])
    own.start()

    lane = lax.broadcasted_iota(jnp.int32, (1, COLS), 1)
    occ_i = jnp.zeros((1, COLS), jnp.float32)
    occ_j = jnp.zeros((1, COLS), jnp.float32)
    for i in range(OCCUPIED):
        occ_i = jnp.where((lane >> 4) == i, occ_ref[i], occ_i)
        occ_j = jnp.where((lane & 15) == i, occ_ref[i], occ_j)
    for s in range(SIDE):
        for t in range(SIDE):
            both = vir_ref[map_ref[0, 0, 0] * SIDE + s] + vir_ref[map_ref[0, 0, 1] * SIDE + t]
            r = s * SIDE + t
            den[r : r + 1, :] = (both - occ_i) - occ_j
    row = lax.broadcasted_iota(jnp.int32, (COLS, COLS), 0)
    col = lax.broadcasted_iota(jnp.int32, (COLS, COLS), 1)
    turn[...] = (((row >> 4) == (col & 15)) & ((row & 15) == (col >> 4))).astype(jnp.bfloat16)

    started = []

    def ring(way, hop, chunk):
        at_y = (y - hop + Y) % Y if way == 0 else (y + hop) % Y
        start, size = CHUNKS[chunk]
        ref = tbuf.at[at_y, core, pl.ds(start, size)]
        return remote(ref, ref, ring_send.at[way, hop, chunk], ring_recv.at[way, hop, chunk], up if way == 0 else down)

    def arrived(way, hop, chunk):
        at_y = (y - hop - 1 + Y) % Y if way == 0 else (y + hop + 1) % Y
        start, size = CHUNKS[chunk]
        ref = tbuf.at[at_y, core, pl.ds(start, size)]
        return remote(ref, ref, ring_send.at[way, hop, chunk], ring_recv.at[way, hop, chunk], up if way == 0 else down)

    def place_y(place):
        step = (0, -1, -2, -3, 1, 2, 3, 4)[place]
        return (y + step + Y) % Y

    def across(place, chunk):
        start, size = CHUNKS[chunk]
        ref = tbuf.at[place_y(place), core, pl.ds(start, size)]
        return remote(ref, ref, core_send.at[place, chunk], core_recv.at[place, chunk], sibling)

    def across_in(place, chunk):
        start, size = CHUNKS[chunk]
        ref = tbuf.at[place_y(place), 1 - core, pl.ds(start, size)]
        return remote(ref, ref, core_send.at[place, chunk], core_recv.at[place, chunk], sibling)

    def go(copy):
        copy.start()
        started.append(copy)

    tin[0].wait_recv()
    for chunk in range(len(CHUNKS)):
        tin[chunk + 1].wait_recv()
        go(ring(0, 0, chunk))
        go(ring(1, 0, chunk))
        go(across(0, chunk))
    for hop in range(1, 4):
        for chunk in range(len(CHUNKS)):
            for way in range(2):
                arrived(way, hop - 1, chunk).wait_recv()
                if hop < 3 or way == LAST_WAY[chunk]:
                    go(ring(way, hop, chunk))
                go(across(hop + 3 * way, chunk))
    own.wait()
    for copy in vout:
        copy.wait_recv()

    def split(value):
        high = value.astype(jnp.bfloat16)
        return high, (value - high.astype(jnp.float32)).astype(jnp.bfloat16)

    def product(v, t):
        v_high, v_low = split(v)
        t_high, t_low = split(t)
        dot = functools.partial(jnp.dot, preferred_element_type=jnp.float32)
        return dot(v_high, t_high) + (dot(v_low, t_high) + dot(v_high, t_low))

    def gathered(tile, tiles):
        return jnp.concatenate([vbuf[pl.ds(tile + k, 8 * ROWS, stride=TILES), :] for k in range(tiles)], axis=1)

    def add(place):
        for chunk in range(len(CHUNKS)):
            across_in(place, chunk).wait_recv()
        at_y = place_y(place)
        t = tbuf[at_y, :, EXTRA:PIECE, :].reshape(2 * MAIN, COLS)
        term = product(gathered(3 * at_y + at_y // 4, 3), t)
        if place == 0:
            acc[...] = term
        else:
            acc[...] += term

    for place in (0, 1, 4, 2, 5):
        add(place)
    for chunk in (0, 2, 1, 3):
        arrived(LAST_WAY[chunk], 3, chunk).wait_recv()
        go(across(7, chunk))
    for place in (3, 6, 7):
        add(place)
    t = tbuf[:, :, 0:EXTRA, :].reshape(128, COLS)
    acc[...] += product(gathered(12, 1), t)

    back = []
    for i, (_, dx, dz) in enumerate(SENDS):
        give[i, 0:ROWS, :] = acc[ROWS * (i + 1) : ROWS * (i + 2), :]
        copy = remote(give.at[i], parts.at[i], part_send.at[i], part_recv.at[i], at(dx=-dx, dz=-dz))
        copy.start()
        back.append(copy)
    total = acc[0:SLOT, :]
    for i in range(7):
        back[i].wait_recv()
        total = total + parts[i]
    mine[...] = total
    swap = remote(mine, other, mir_send.at[0], mir_recv.at[0], twin)
    swap.start()
    swap.wait_recv()
    dot = functools.partial(jnp.dot, preferred_element_type=jnp.float32)
    high, rest = split(other[...])
    mid = (other[...] - high.astype(jnp.float32)) - rest.astype(jnp.float32)
    turned = (dot(high, turn[...]) + dot(rest, turn[...])) + dot(mid.astype(jnp.bfloat16), turn[...])
    for s in range(SIDE):
        for t in range(SIDE):
            r, q = s * SIDE + t, t * SIDE + s
            out_ref[r] = (total[r : r + 1] + turned[q : q + 1]) / den[r : r + 1, :]

    for copy in tin + vout + started + back + [swap]:
        copy.wait_send()


def body(integrals, amplitudes, block_map, eps_vir, eps_occ):
    smem = pl.BlockSpec(memory_space=pltpu.SMEM)
    hbm = pl.BlockSpec(memory_space=pltpu.HBM)
    dma = pltpu.SemaphoreType.DMA
    f32 = jnp.float32
    tiles = jnp.transpose(integrals, (0, 2, 1, 3)).reshape(ROWS, 8 * TILES, 1, LANES)
    update = pl.pallas_call(
        kernel,
        out_shape=jax.ShapeDtypeStruct((ROWS, 1, COLS), f32),
        in_specs=[hbm, hbm, smem, smem, smem],
        out_specs=pl.BlockSpec(memory_space=pltpu.VMEM),
        scratch_shapes=[
            pltpu.VMEM((8 * ROWS * TILES, LANES), f32),
            pltpu.VMEM((8, 2, PIECE, COLS), f32),
            pltpu.VMEM((8 * ROWS, COLS), f32),
            pltpu.VMEM((7, SLOT, COLS), f32),
            pltpu.VMEM((7, SLOT, COLS), f32),
            pltpu.VMEM((SLOT, COLS), f32),
            pltpu.VMEM((SLOT, COLS), f32),
            pltpu.VMEM((SLOT, COLS), f32),
            pltpu.VMEM((COLS, COLS), jnp.bfloat16),
            dma((5,)), dma((5,)),
            dma((2, 4, 4)), dma((2, 4, 4)),
            dma((8, 4)), dma((8, 4)),
            dma((7,)), dma((7,)), dma((1,)),
            dma((8,)), dma((8,)),
            dma((8,)), dma((8,)),
        ],
        compiler_params=pltpu.CompilerParams(
            collective_id=0, has_side_effects=True, vmem_limit_bytes=56 * 2**20
        ),
        name="ladder",
    )(tiles, amplitudes, block_map, eps_vir, eps_occ)
    return jnp.transpose(update.reshape(1, ROWS, 1, COLS), (0, 2, 1, 3))


def solution(mesh):
    in_specs = (P("blk", "pair", None, None), P("blk", None), P("blk", "pair", None), P(), P())
    out_specs = P("blk", "pair", None, None)
    return jax.shard_map(body, mesh=mesh, in_specs=in_specs, out_specs=out_specs, check_vma=False)
```

time: 56.6 us -> 53 us (0.936)
  Pallas kernels: 53.4 us -> 51.4 us
  local copies, waits for them, and re-layouts: 3.03 us -> 1.35 us
    pallas_call x1, Pallas kernels: 53.4 us -> 51.4 us  [body(): pl.pallas_call(kernel, out_shape=jax.ShapeDtypeStruct((ROWS, 1, COLS), f3...]
    unnamed x9 -> x1, local copies, waits for them, and re-layouts: 2.39 us -> 1.35 us
    pallas_call x1 -> x0, local copies, waits for them, and re-layouts: 0.64 us -> none  [body(): pl.pallas_call(kernel, out_shape=jax.ShapeDtypeStruct((1, 1, ROWS, COLS),...]
where the time goes in v2:
time: 53 us; the launch traced here: 52.8 us
  Pallas kernels  51.4 us (97%)
  local copies, waits for them, and re-layouts  1.35 us (3%)
    pallas_call x1, Pallas kernels, body(): pl.pallas_call(kernel, out_shape=jax.ShapeDtypeStruct((ROWS, 1, COLS), f3...  51.4 us
    unnamed x1, local copies, waits for them, and re-layouts  1.35 us

profile of v2, /device:TPU:2, one launch (start us, length us, event | category | flops | bytes accessed | tf_op | source)
XLA Modules:
  0.0 52.8 jit_solution(4537290233467445684)
XLA Ops:
  0.0 51.4 %ladder.1 = f32[25,1,256]{2,1,0:T(1,128)} custom-call(f32[25,200,1,128]{3,2,1,0:T(1,128)} %bitcast.4, f32[1600,256]{1,0:T(8,128)} %t_ref.1, s32[1,1,2]{2,1,0:T(1,128)} %map_ref.1, f32[160]{0:T(256)} %vir_ref.1, f32[16]{0:T(128)} %occ_ref.1), custom_call_target="tpu_custom_call" | custom-call | tf_op jit(solution)/shard_map/ladder/pallas_call | solution.py:223
  51.4 1.4 %copy.8 = f32[1,1,25,256]{3,1,2,0:T(1,128)} copy(f32[1,1,25,256]{3,1,2,0:T(1,128)} %bitcast.5) | data formatting | bytes 51200

commit v3 on v2

v3 whole, which is shorter than its diff:
```python
import functools

import jax
import jax.numpy as jnp
from jax import lax
from jax.experimental import pallas as pl
from jax.experimental.pallas import tpu as pltpu
from jax.sharding import PartitionSpec as P

MESH = pl.DeviceIdType.MESH

OCCUPIED = 16
SIDE = 5
ROWS = 25
SLOT = 32
COLS = 256
LANES = 128
TILES = 25
LAYERS = 8
PIECE = 192
PART = 64
X, Y, Z = 4, 8, 8
SENDS = ((2, 1, 0), (6, -1, 0), (3, 0, 1), (5, 0, -1), (1, -1, 1), (7, 1, -1), (4, 2, 0))
RETURNS = (6, 4, 5, 0, 1, 2, 3)
PLACES = (0, -1, -2, -3, 1, 2, 3, 4)


def device(z, y, x, core):
    return (z * 2 + y // 4, (y % 4) * 8 + x * 2 + core)


def share(layer, colour):
    low = 2 - (layer + colour) % 2
    start_low = 3 * (colour // 2) + (colour % 2) * (3 - low)
    start_high = 3 * (colour // 2) + (colour % 2) * low
    return low, start_low, start_high


def tile_places(parity):
    places = {}
    for colour in range(8):
        low, start_low, start_high = share(parity, colour)
        for i in range(low):
            places[start_low + i] = (colour, i)
        for i in range(3 - low):
            places[13 + start_high + i] = (colour, low + i)
    return places


def kernel(
    v_ref, t_ref, map_hbm, vir_hbm, occ_hbm, out_ref,
    map_ref, vir_ref, occ_ref, small,
    raw, packed, vbuf, tbuf, tlast, acc, give, parts, mine, other, den, turn,
    ready, raw_sem, tin_send, tin_recv, ring_send, ring_recv, core_send, core_recv,
    last_send, last_recv, last_across,
    v_send, v_recv, v_own, part_send, part_recv, mir_send, mir_recv,
):
    blk, pair = lax.axis_index("blk"), lax.axis_index("pair")
    z, y_hi = blk // 2, blk % 2
    y_lo, x, core = pair // 8, (pair // 2) % 4, pair % 2
    y = y_hi * 4 + y_lo
    colour = (3 * y + 2 * x) % 8
    partner_colour = (3 * (7 - y) + 2 * x) % 8

    def at(dx=0, dy=0, dz=0):
        return device((z + dz + Z) % Z, (y + dy + Y) % Y, (x + dx + X) % X, core)

    sibling = device(z, y, x, 1 - core)
    up, down = at(dz=1), at(dz=-1)
    twin = at(dy=2 - 4 * (y_lo // 2))
    partner = device(z, 7 - y, x, core)

    load = pltpu.make_async_copy(v_ref, raw.reshape(ROWS, LAYERS * TILES, 1, LANES), raw_sem.at[0])
    load.start()
    tables = [
        pltpu.make_async_copy(src, dst, small.at[n])
        for n, (src, dst) in enumerate(((map_hbm, map_ref), (vir_hbm, vir_ref), (occ_hbm, occ_ref)))
    ]
    for copy in tables:
        copy.start()

    barrier = pltpu.get_barrier_semaphore()
    greet = [sibling, twin, partner] + [at(dx=-dx, dy=-dy) for _, dx, dy in SENDS]

    def signal(semaphore, peer):
        pl.semaphore_signal(semaphore, inc=1, device_id=peer, device_id_type=MESH)

    for peer in greet:
        signal(barrier, peer)
    pl.when(z < Z - 1)(lambda: signal(barrier, up))
    pl.when(z == 0)(lambda: signal(barrier, down))
    load.wait()

    def pack(pairs, carry):
        for parity in range(2):
            layer = 2 * pairs + parity
            for tile, (of_colour, place) in sorted(tile_places(parity).items()):
                value = raw[pl.ds(TILES * layer + tile, ROWS, stride=LAYERS * TILES), :]
                packed[pl.ds(of_colour * ROWS * TILES + 3 * layer + place, ROWS, stride=TILES), :] = value
            value = raw[pl.ds(TILES * layer + 12, ROWS, stride=LAYERS * TILES), :]
            packed[pl.ds(layer * ROWS * TILES + 24, ROWS, stride=TILES), :] = value
        return carry

    lax.fori_loop(0, LAYERS // 2, pack, 0)

    lower = (z + Z - 1) // Z + z // (Z - 1)
    pl.semaphore_wait(barrier, len(greet) + lower)
    pl.when(z > 0)(lambda: signal(ready.at[0], down))
    pl.when(z == Z - 1)(lambda: signal(ready.at[1], up))

    started = []

    def remote(src, dst, send, recv, peer):
        return pltpu.make_async_remote_copy(
            src_ref=src, dst_ref=dst, send_sem=send, recv_sem=recv, device_id=peer, device_id_type=MESH
        )

    def go(copy):
        copy.start()
        started.append(copy)

    def landed(ref, sem):
        pltpu.make_async_copy(ref, ref, sem).wait()

    def held(of_colour):
        low, start_low, start_high = share(z, of_colour)
        always = (1 - y_hi) * 128 * start_low + y_hi * (64 + 128 * (start_high + 2 - low))
        middle = (1 - y_hi) * 128 * (start_low + 1) + y_hi * (64 + 128 * start_high)
        rows = [t_ref.at[pl.ds(pl.multiple_of(first + PART * core, PART), PART)] for first in (always, middle)]
        return rows, low + y_hi == 2

    def tile_rows(layer, tile):
        k = (2 * y_hi, 1, 2 - 2 * y_hi)[tile]
        return tbuf.at[layer, core, pl.ds(pl.multiple_of(PART * k, PART), PART)]

    own_rows, own_middle = held(colour)
    out_rows, out_middle = held(partner_colour)
    partner_part = tile_rows(z, 0)
    middle_out = remote(out_rows[1], tile_rows(z, 1), tin_send.at[1], tin_recv.at[1], partner)
    first_up = remote(own_rows[0], tile_rows(z, 0), ring_send.at[0, 0, 0], ring_recv.at[0, 0, 0], up)
    first_down = remote(own_rows[0], tile_rows(z, 0), ring_send.at[1, 0, 0], ring_recv.at[1, 0, 0], down)
    pl.when(z > 0)(first_down.start)
    pl.when(z == Z - 1)(first_up.start)
    go(remote(out_rows[0], partner_part, tin_send.at[2], tin_recv.at[2], partner))
    pl.when(out_middle)(middle_out.start)
    native = pltpu.make_async_copy(own_rows[0], tile_rows(z, 0), tin_recv.at[0])
    native.start()
    pl.when(own_middle)(pltpu.make_async_copy(own_rows[1], tile_rows(z, 1), tin_recv.at[1]).start)

    ahead = (z - colour + Z) % Z
    last = tlast.at[pl.ds(pl.multiple_of(PART * core, PART), PART)]
    last_rows = t_ref.at[pl.ds(pl.multiple_of((1 - core) * 1536, PART), PART)]
    last_out = remote(last_rows, last, last_send.at[2], last_recv.at[0], partner)
    sends_last = (partner_colour == z) & (y_hi == core)
    pl.when(sends_last)(last_out.start)
    pl.when((ahead == 0) & (y_hi == core))(pltpu.make_async_copy(last_rows, last, last_recv.at[0]).start)
    last_up = remote(last, last, last_send.at[0], last_recv.at[0], up)
    last_down = remote(last, last, last_send.at[1], last_recv.at[0], down)
    last_over = remote(last, last, last_send.at[3], last_across.at[0], sibling)

    def pass_last(hop):
        if hop == 0:
            @pl.when(ahead == 0)
            def _():
                landed(last, last_recv.at[0])
                last_up.start()
                last_down.start()
                last_over.start()
            return

        if hop < 4:
            @pl.when(ahead == hop)
            def _():
                landed(last, last_recv.at[0])
                if hop < 3:
                    last_up.start()
                last_over.start()

        @pl.when(ahead == Z - hop)
        def _():
            landed(last, last_recv.at[0])
            if hop < 4:
                last_down.start()
            last_over.start()

    slots = vbuf.reshape(8, ROWS, TILES, 1, LANES)
    sorted_v = packed.reshape(8, ROWS, TILES, 1, LANES)
    vout = []
    for i, (step, dx, dy) in enumerate(SENDS):
        src = sorted_v.at[(colour + step) % 8]
        vout.append(remote(src, slots.at[i + 1], v_send.at[i], v_recv.at[i], at(dx=dx, dy=dy)))
        vout[-1].start()
    own = pltpu.make_async_copy(sorted_v.at[colour], slots.at[0], v_own.at[0])
    own.start()

    for copy in tables:
        copy.wait()
    lane = lax.broadcasted_iota(jnp.int32, (1, COLS), 1)
    occ_i = jnp.zeros((1, COLS), jnp.float32)
    occ_j = jnp.zeros((1, COLS), jnp.float32)
    for i in range(OCCUPIED):
        occ_i = jnp.where((lane >> 4) == i, occ_ref[i], occ_i)
        occ_j = jnp.where((lane & 15) == i, occ_ref[i], occ_j)
    for s in range(SIDE):
        for t in range(SIDE):
            both = vir_ref[map_ref[0, 0, 0] * SIDE + s] + vir_ref[map_ref[0, 0, 1] * SIDE + t]
            r = s * SIDE + t
            den[r : r + 1, :] = (both - occ_i) - occ_j
    row = lax.broadcasted_iota(jnp.int32, (COLS, COLS), 0)
    col = lax.broadcasted_iota(jnp.int32, (COLS, COLS), 1)
    turn[...] = (((row >> 4) == (col & 15)) & ((row & 15) == (col >> 4))).astype(jnp.bfloat16)

    def layer_of(place):
        return (z + PLACES[place] + Z) % Z

    def ring(way, hop, role):
        ref = tile_rows((z - hop + Z) % Z if way == 0 else (z + hop) % Z, role)
        return remote(ref, ref, ring_send.at[way, hop, role], ring_recv.at[way, hop, role], up if way == 0 else down)

    def arrived(way, hop, role):
        landed(tile_rows(layer_of(hop + 1 + 3 * way if hop < 3 else 7), role), ring_recv.at[way, hop, role])

    def across(place):
        ref = tbuf.at[layer_of(place), core]
        return remote(ref, ref, core_send.at[place], core_recv.at[place], sibling)

    @pl.when(z < Z - 1)
    def _():
        pl.semaphore_wait(ready.at[0], 1)
        first_up.start()

    for role in (2, 1):
        landed(tile_rows(z, role), tin_recv.at[role])
        go(ring(0, 0, role))

    @pl.when(z == 0)
    def _():
        pl.semaphore_wait(ready.at[1], 1)
        first_down.start()

    for role in (2, 1):
        go(ring(1, 0, role))
    native.wait()
    go(across(0))
    pass_last(0)
    for hop in range(1, 3):
        for role in (0, 2, 1):
            for way in (1, 0):
                arrived(way, hop - 1, role)
                go(ring(way, hop, role))
        for way in (1, 0):
            go(across(hop + 3 * way))
        pass_last(hop)
    for role in (0, 2, 1):
        arrived(1, 2, role)
        go(ring(1, 3, role))
    go(across(6))

    own.wait()
    for copy in vout:
        copy.wait_recv()

    def split(value):
        high = value.astype(jnp.bfloat16)
        return high, (value - high.astype(jnp.float32)).astype(jnp.bfloat16)

    def product(v, t):
        v_high, v_low = split(v)
        t_high, t_low = split(t)
        dot = functools.partial(jnp.dot, preferred_element_type=jnp.float32)
        return dot(v_high, t_high) + (dot(v_low, t_high) + dot(v_high, t_low))

    def gathered(tile, tiles):
        return jnp.concatenate([vbuf[pl.ds(tile + k, 8 * ROWS, stride=TILES), :] for k in range(tiles)], axis=1)

    def add(place):
        layer = layer_of(place)
        landed(tbuf.at[layer, 1 - core], core_recv.at[place])
        t = [tbuf[layer, c, PART * k : PART * (k + 1), :] for k in range(3) for c in range(2)]
        term = product(gathered(3 * layer, 3), jnp.concatenate(t, axis=0))
        if place == 0:
            acc[...] = term
        else:
            acc[...] += term

    for place in (0, 4, 1, 5, 2):
        add(place)
    for role in (0, 2, 1):
        arrived(0, 2, role)
    go(across(3))
    pass_last(3)
    for role in (0, 2, 1):
        arrived(1, 3, role)
    go(across(7))
    pass_last(4)
    for place in (6, 3, 7):
        add(place)
    landed(tlast.at[pl.ds(pl.multiple_of(PART * (1 - core), PART), PART)], last_across.at[0])
    final = acc[...] + product(gathered(24, 1), tlast[...])

    back = []
    for i in RETURNS:
        _, dx, dy = SENDS[i]
        give[i, 0:ROWS, :] = final[ROWS * (i + 1) : ROWS * (i + 2), :]
        copy = remote(give.at[i], parts.at[i], part_send.at[i], part_recv.at[i], at(dx=-dx, dy=-dy))
        copy.start()
        back.append(copy)

    for copy in vout + started:
        copy.wait_send()
    pl.when(out_middle)(middle_out.wait_send)
    pl.when(sends_last)(last_out.wait_send)
    pl.when(ahead < 3)(last_up.wait_send)
    pl.when((ahead == 0) | (ahead > 4))(last_down.wait_send)
    first_up.wait_send()
    first_down.wait_send()
    last_over.wait_send()
    total = final[0:SLOT, :]
    for i in range(7):
        back[i].wait_recv()
        total = total + parts[RETURNS[i]]
    mine[...] = total
    swap = remote(mine, other, mir_send.at[0], mir_recv.at[0], twin)
    swap.start()
    for copy in back:
        copy.wait_send()
    swap.wait_recv()
    dot = functools.partial(jnp.dot, preferred_element_type=jnp.float32)
    high, rest = split(other[...])
    mid = (other[...] - high.astype(jnp.float32)) - rest.astype(jnp.float32)
    turned = (dot(high, turn[...]) + dot(rest, turn[...])) + dot(mid.astype(jnp.bfloat16), turn[...])
    for s in range(SIDE):
        for t in range(SIDE):
            r, q = s * SIDE + t, t * SIDE + s
            out_ref[r] = (total[r : r + 1] + turned[q : q + 1]) / den[r : r + 1, :]

    swap.wait_send()


def body(integrals, amplitudes, block_map, eps_vir, eps_occ):
    hbm = pl.BlockSpec(memory_space=pltpu.HBM)
    dma = pltpu.SemaphoreType.DMA
    f32 = jnp.float32
    tiles = jnp.transpose(integrals, (0, 2, 1, 3)).reshape(ROWS, 8 * TILES, 1, LANES)
    update = pl.pallas_call(
        kernel,
        out_shape=jax.ShapeDtypeStruct((ROWS, 1, COLS), f32),
        in_specs=[hbm] * 5,
        out_specs=pl.BlockSpec(memory_space=pltpu.VMEM),
        scratch_shapes=[
            pltpu.SMEM((1, 1, 2), jnp.int32),
            pltpu.SMEM((160,), f32),
            pltpu.SMEM((16,), f32),
            dma((3,)),
            pltpu.VMEM((8 * ROWS * TILES, LANES), f32),
            pltpu.VMEM((8 * ROWS * TILES, LANES), f32),
            pltpu.VMEM((8 * ROWS * TILES, LANES), f32),
            pltpu.VMEM((LAYERS, 2, PIECE, COLS), f32),
            pltpu.VMEM((128, COLS), f32),
            pltpu.VMEM((8 * ROWS, COLS), f32),
            pltpu.VMEM((7, SLOT, COLS), f32),
            pltpu.VMEM((7, SLOT, COLS), f32),
            pltpu.VMEM((SLOT, COLS), f32),
            pltpu.VMEM((SLOT, COLS), f32),
            pltpu.VMEM((SLOT, COLS), f32),
            pltpu.VMEM((COLS, COLS), jnp.bfloat16),
            pltpu.SemaphoreType.REGULAR((2,)),
            dma((1,)), dma((3,)), dma((3,)),
            dma((2, 4, 3)), dma((2, 4, 3)),
            dma((8,)), dma((8,)),
            dma((4,)), dma((1,)), dma((1,)),
            dma((7,)), dma((7,)), dma((1,)),
            dma((8,)), dma((8,)),
            dma((8,)), dma((8,)),
        ],
        compiler_params=pltpu.CompilerParams(
            collective_id=0, has_side_effects=True, vmem_limit_bytes=56 * 2**20
        ),
        name="ladder",
    )(tiles, amplitudes, block_map, eps_vir, eps_occ)
    return jnp.transpose(update.reshape(1, ROWS, 1, COLS), (0, 2, 1, 3))


def solution(mesh):
    in_specs = (P("blk", "pair", None, None), P("blk", None), P("blk", "pair", None), P(), P())
    out_specs = P("blk", "pair", None, None)
    return jax.shard_map(body, mesh=mesh, in_specs=in_specs, out_specs=out_specs, check_vma=False)
```

time: 53 us -> 50.4 us (0.951)
  the two profiles are of different devices: /device:TPU:2 before, /device:TPU:192 now
where the time goes in v3:
time: 50.4 us; the launch traced here: 50.2 us
  Pallas kernels  48.8 us (97%)
  local copies, waits for them, and re-layouts  1.35 us (3%)
    pallas_call x1, Pallas kernels, body(): pl.pallas_call(kernel, out_shape=jax.ShapeDtypeStruct((ROWS, 1, COLS), f3...  48.8 us
    unnamed x1, local copies, waits for them, and re-layouts  1.35 us

profile of v3, /device:TPU:192, one launch (start us, length us, event | category | flops | bytes accessed | tf_op | source)
XLA Modules:
  0.0 50.2 jit_solution(9887173955597290888)
XLA Ops:
  0.0 48.8 %ladder.1 = f32[25,1,256]{2,1,0:T(1,128)} custom-call(f32[25,200,1,128]{3,2,1,0:T(1,128)} %bitcast.4, f32[1600,256]{1,0:T(8,128)} %t_ref.1, s32[1,1,2]{2,1,0:T(1,128)} %map_hbm.1, f32[160]{0:T(256)} %vir_hbm.1, f32[16]{0:T(128)} %occ_hbm.1), custom_call_target="tpu_custom_call" | custom-call | tf_op jit(solution)/shard_map/ladder/pallas_call | solution.py:345
  48.8 1.4 %copy.8 = f32[1,1,25,256]{3,1,2,0:T(1,128)} copy(f32[1,1,25,256]{3,1,2,0:T(1,128)} %bitcast.5) | data formatting | bytes 51200

commit v4 on v3

--- a/solution.py
+++ b/solution.py
@@ -89,20 +89,6 @@
         signal(barrier, peer)
     pl.when(z < Z - 1)(lambda: signal(barrier, up))
     pl.when(z == 0)(lambda: signal(barrier, down))
-    load.wait()
-
-    def pack(pairs, carry):
-        for parity in range(2):
-            layer = 2 * pairs + parity
-            for tile, (of_colour, place) in sorted(tile_places(parity).items()):
-                value = raw[pl.ds(TILES * layer + tile, ROWS, stride=LAYERS * TILES), :]
-                packed[pl.ds(of_colour * ROWS * TILES + 3 * layer + place, ROWS, stride=TILES), :] = value
-            value = raw[pl.ds(TILES * layer + 12, ROWS, stride=LAYERS * TILES), :]
-            packed[pl.ds(layer * ROWS * TILES + 24, ROWS, stride=TILES), :] = value
-        return carry
-
-    lax.fori_loop(0, LAYERS // 2, pack, 0)
-
     lower = (z + Z - 1) // Z + z // (Z - 1)
     pl.semaphore_wait(barrier, len(greet) + lower)
     pl.when(z > 0)(lambda: signal(ready.at[0], down))
@@ -125,7 +111,7 @@
     def held(of_colour):
         low, start_low, start_high = share(z, of_colour)
         always = (1 - y_hi) * 128 * start_low + y_hi * (64 + 128 * (start_high + 2 - low))
-        middle = (1 - y_hi) * 128 * (start_low + 1) + y_hi * (64 + 128 * start_high)
+        middle = (1 - y_hi) * 128 * (start_low + low - 1) + y_hi * (64 + 128 * start_high)
         rows = [t_ref.at[pl.ds(pl.multiple_of(first + PART * core, PART), PART)] for first in (always, middle)]
         return rows, low + y_hi == 2
 
@@ -183,32 +169,30 @@
                 last_down.start()
             last_over.start()
 
+    load.wait()
+
+    def pack(pairs, carry):
+        for parity in range(2):
+            layer = 2 * pairs + parity
+            for tile, (of_colour, place) in sorted(tile_places(parity).items()):
+                value = raw[pl.ds(TILES * layer + tile, ROWS, stride=LAYERS * TILES), :]
+                packed[pl.ds(of_colour * ROWS * TILES + 3 * layer + place, ROWS, stride=TILES), :] = value
+            value = raw[pl.ds(TILES * layer + 12, ROWS, stride=LAYERS * TILES), :]
+            packed[pl.ds(layer * ROWS * TILES + 24, ROWS, stride=TILES), :] = value
+        return carry
+
+    lax.fori_loop(0, LAYERS // 2, pack, 0)
+
     slots = vbuf.reshape(8, ROWS, TILES, 1, LANES)
     sorted_v = packed.reshape(8, ROWS, TILES, 1, LANES)
     vout = []
-    for i, (step, dx, dy) in enumerate(SENDS):
+    for i in RETURNS:
+        step, dx, dy = SENDS[i]
         src = sorted_v.at[(colour + step) % 8]
         vout.append(remote(src, slots.at[i + 1], v_send.at[i], v_recv.at[i], at(dx=dx, dy=dy)))
         vout[-1].start()
     own = pltpu.make_async_copy(sorted_v.at[colour], slots.at[0], v_own.at[0])
     own.start()
-
-    for copy in tables:
-        copy.wait()
-    lane = lax.broadcasted_iota(jnp.int32, (1, COLS), 1)
-    occ_i = jnp.zeros((1, COLS), jnp.float32)
-    occ_j = jnp.zeros((1, COLS), jnp.float32)
-    for i in range(OCCUPIED):
-        occ_i = jnp.where((lane >> 4) == i, occ_ref[i], occ_i)
-        occ_j = jnp.where((lane & 15) == i, occ_ref[i], occ_j)
-    for s in range(SIDE):
-        for t in range(SIDE):
-            both = vir_ref[map_ref[0, 0, 0] * SIDE + s] + vir_ref[map_ref[0, 0, 1] * SIDE + t]
-            r = s * SIDE + t
-            den[r : r + 1, :] = (both - occ_i) - occ_j
-    row = lax.broadcasted_iota(jnp.int32, (COLS, COLS), 0)
-    col = lax.broadcasted_iota(jnp.int32, (COLS, COLS), 1)
-    turn[...] = (((row >> 4) == (col & 15)) & ((row & 15) == (col >> 4))).astype(jnp.bfloat16)
 
     def layer_of(place):
         return (z + PLACES[place] + Z) % Z
@@ -299,12 +283,33 @@
     final = acc[...] + product(gathered(24, 1), tlast[...])
 
     back = []
+    give_rows = give.reshape(7, ROWS, 2, 1, LANES)
+    part_rows = parts.reshape(7, ROWS, 2, 1, LANES)
     for i in RETURNS:
         _, dx, dy = SENDS[i]
-        give[i, 0:ROWS, :] = final[ROWS * (i + 1) : ROWS * (i + 2), :]
-        copy = remote(give.at[i], parts.at[i], part_send.at[i], part_recv.at[i], at(dx=-dx, dy=-dy))
+        for half in range(2):
+            value = final[ROWS * (i + 1) : ROWS * (i + 2), LANES * half : LANES * (half + 1)]
+            give[pl.ds(2 * ROWS * i + half, ROWS, stride=2), :] = value
+        copy = remote(give_rows.at[i], part_rows.at[i], part_send.at[i], part_recv.at[i], at(dx=-dx, dy=-dy))
         copy.start()
         back.append(copy)
+
+    for copy in tables:
+        copy.wait()
+    lane = lax.broadcasted_iota(jnp.int32, (1, COLS), 1)
+    occ_i = jnp.zeros((1, COLS), jnp.float32)
+    occ_j = jnp.zeros((1, COLS), jnp.float32)
+    for i in range(OCCUPIED):
+        occ_i = jnp.where((lane >> 4) == i, occ_ref[i], occ_i)
+        occ_j = jnp.where((lane & 15) == i, occ_ref[i], occ_j)
+    for s in range(SIDE):
+        for t in range(SIDE):
+            both = vir_ref[map_ref[0, 0, 0] * SIDE + s] + vir_ref[map_ref[0, 0, 1] * SIDE + t]
+            r = s * SIDE + t
+            den[r : r + 1, :] = (both - occ_i) - occ_j
+    row = lax.broadcasted_iota(jnp.int32, (COLS, COLS), 0)
+    col = lax.broadcasted_iota(jnp.int32, (COLS, COLS), 1)
+    turn[...] = (((row >> 4) == (col & 15)) & ((row & 15) == (col >> 4))).astype(jnp.bfloat16)
 
     for copy in vout + started:
         copy.wait_send()
@@ -315,11 +320,13 @@
     first_up.wait_send()
     first_down.wait_send()
     last_over.wait_send()
-    total = final[0:SLOT, :]
+    total = final[0:ROWS, :]
     for i in range(7):
         back[i].wait_recv()
-        total = total + parts[RETURNS[i]]
-    mine[...] = total
+        n = 2 * ROWS * RETURNS[i]
+        halves = [parts[pl.ds(n + half, ROWS, stride=2), :] for half in range(2)]
+        total = total + jnp.concatenate(halves, axis=1)
+    mine[0:ROWS, :] = total
     swap = remote(mine, other, mir_send.at[0], mir_recv.at[0], twin)
     swap.start()
     for copy in back:
@@ -358,8 +365,8 @@
             pltpu.VMEM((LAYERS, 2, PIECE, COLS), f32),
             pltpu.VMEM((128, COLS), f32),
             pltpu.VMEM((8 * ROWS, COLS), f32),
-            pltpu.VMEM((7, SLOT, COLS), f32),
-            pltpu.VMEM((7, SLOT, COLS), f32),
+            pltpu.VMEM((7 * ROWS * 2, LANES), f32),
+            pltpu.VMEM((7 * ROWS * 2, LANES), f32),
             pltpu.VMEM((SLOT, COLS), f32),
             pltpu.VMEM((SLOT, COLS), f32),
             pltpu.VMEM((SLOT, COLS), f32),

time: 50.4 us -> 49.8 us (0.988)
  the two profiles are of different devices: /device:TPU:192 before, /device:TPU:8 now
where the time goes in v4:
time: 49.8 us; the launch traced here: 49.5 us
  Pallas kernels  48.2 us (97%)
  local copies, waits for them, and re-layouts  1.35 us (3%)
    pallas_call x1, Pallas kernels, body(): pl.pallas_call(kernel, out_shape=jax.ShapeDtypeStruct((ROWS, 1, COLS), f3...  48.2 us
    unnamed x1, local copies, waits for them, and re-layouts  1.35 us

profile of v4, /device:TPU:8, one launch (start us, length us, event | category | flops | bytes accessed | tf_op | source)
XLA Modules:
  0.0 49.5 jit_solution(1397171775342599700)
XLA Ops:
  0.0 48.2 %ladder.1 = f32[25,1,256]{2,1,0:T(1,128)} custom-call(f32[25,200,1,128]{3,2,1,0:T(1,128)} %bitcast.4, f32[1600,256]{1,0:T(8,128)} %t_ref.1, s32[1,1,2]{2,1,0:T(1,128)} %map_hbm.1, f32[160]{0:T(256)} %vir_hbm.1, f32[16]{0:T(128)} %occ_hbm.1), custom_call_target="tpu_custom_call" | custom-call | tf_op jit(solution)/shard_map/ladder/pallas_call | solution.py:352
  48.2 1.4 %copy.8 = f32[1,1,25,256]{3,1,2,0:T(1,128)} copy(f32[1,1,25,256]{3,1,2,0:T(1,128)} %bitcast.5) | data formatting | bytes 51200

commit v5 on v4

--- a/solution.py
+++ b/solution.py
@@ -262,6 +262,8 @@
         landed(tbuf.at[layer, 1 - core], core_recv.at[place])
         t = [tbuf[layer, c, PART * k : PART * (k + 1), :] for k in range(3) for c in range(2)]
         term = product(gathered(3 * layer, 3), jnp.concatenate(t, axis=0))
+        if place == 7:
+            return acc[...] + term
         if place == 0:
             acc[...] = term
         else:
@@ -277,10 +279,11 @@
         arrived(1, 3, role)
     go(across(7))
     pass_last(4)
-    for place in (6, 3, 7):
+    for place in (6, 3):
         add(place)
     landed(tlast.at[pl.ds(pl.multiple_of(PART * (1 - core), PART), PART)], last_across.at[0])
-    final = acc[...] + product(gathered(24, 1), tlast[...])
+    acc[...] += product(gathered(24, 1), tlast[...])
+    final = add(7)
 
     back = []
     give_rows = give.reshape(7, ROWS, 2, 1, LANES)

time: 49.8 us -> 50.1 us (level)
  no operation moved by 1% of the time
where the time goes in v5:
time: 50.1 us; the launch traced here: 49.9 us
  Pallas kernels  48.6 us (97%)
  local copies, waits for them, and re-layouts  1.35 us (3%)
    pallas_call x1, Pallas kernels, body(): pl.pallas_call(kernel, out_shape=jax.ShapeDtypeStruct((ROWS, 1, COLS), f3...  48.6 us
    unnamed x1, local copies, waits for them, and re-layouts  1.35 us

profile of v5, /device:TPU:8, one launch (start us, length us, event | category | flops | bytes accessed | tf_op | source)
XLA Modules:
  0.0 49.9 jit_solution(2187794068213168032)
XLA Ops:
  0.0 48.6 %ladder.1 = f32[25,1,256]{2,1,0:T(1,128)} custom-call(f32[25,200,1,128]{3,2,1,0:T(1,128)} %bitcast.4, f32[1600,256]{1,0:T(8,128)} %t_ref.1, s32[1,1,2]{2,1,0:T(1,128)} %map_hbm.1, f32[160]{0:T(256)} %vir_hbm.1, f32[16]{0:T(128)} %occ_hbm.1), custom_call_target="tpu_custom_call" | custom-call | tf_op jit(solution)/shard_map/ladder/pallas_call | solution.py:355
  48.6 1.4 %copy.8 = f32[1,1,25,256]{3,1,2,0:T(1,128)} copy(f32[1,1,25,256]{3,1,2,0:T(1,128)} %bitcast.5) | data formatting | bytes 51200
